TPU v7x, 256 devices: a whole 4x4x8 slice. The times are simulated.
256 devices in a mesh: dp: 2 (over core), seq: 32 (over y, z_lo, x), heads: 4 (over z_hi).
Axes of the slice: x: 4, y: 4, z: 8 (z_hi: 4, z_lo: 2; z = z_hi * 2 + z_lo), core: 2. Of those that a mesh axis runs over, the one named last changes fastest.
Arguments:
- frames_in: bfloat16 [2, 32, 512, 2048], P('dp', 'seq'), may hold values from -80 to 80
- w_query: bfloat16 [2048, 2048], P(('dp', 'seq'), 'heads'), may hold values from -0.125 to 0.125
- w_key: bfloat16 [2048, 2048], P(('dp', 'seq'), 'heads'), may hold values from -0.125 to 0.125
- w_value: bfloat16 [2048, 2048], P(('dp', 'seq'), 'heads'), may hold values from -0.125 to 0.125
- w_out: bfloat16 [2048, 2048], P('heads', ('dp', 'seq')), may hold values from -0.125 to 0.125
- grad_in: bfloat16 [2, 32, 512, 2048], P('dp', 'seq'), may hold values from -6 to 6
Outputs:
- grad_frames: bfloat16 [2, 32, 512, 2048], P('dp', 'seq', None, 'heads')
- grad_query: bfloat16 [2048, 2048], P(('dp', 'seq'), 'heads')
- grad_key: bfloat16 [2048, 2048], P(('dp', 'seq'), 'heads')
- grad_value: bfloat16 [2048, 2048], P(('dp', 'seq'), 'heads')
- grad_out: bfloat16 [2048, 2048], P('heads', ('dp', 'seq'))
All inputs are finite; a program needn't handle non-finite values.
Results may differ from a plain program's by a relative error of at most 0.018.
Values may be sent and summed in bfloat16 or wider, within the bound.
No kernel may reach another device: no remote copies, remote signals or barrier semaphores. Data moves between devices by JAX's collectives and lax.ppermute only.
A program may use at most 128 MiB of HBM per device.

v0:
```python
import jax
import jax.numpy as jnp
from jax import lax
from jax.sharding import PartitionSpec as P

HD = 128


EPS = 1e-06


def norm_heads(t):
    split = t.reshape(t.shape[:-1] + (t.shape[-1] // HD, HD))
    scaled = split * lax.rsqrt(jnp.mean(split * split, axis=-1, keepdims=True) + EPS)
    return scaled.reshape(t.shape)


def contract_rows(left, right):
    return lax.dot_general(
        left, right, (((0,), (0,)), ((), ())), preferred_element_type=jnp.float32
    )


def contract_cols(left, right):
    return lax.dot_general(
        left, right, (((1,), (1,)), ((), ())), preferred_element_type=jnp.float32
    )


def to_heads(t):
    return t.reshape(t.shape[1], t.shape[2], t.shape[3] // HD, HD)


def from_heads(t):
    return t.reshape((1, t.shape[0], t.shape[1], t.shape[2] * t.shape[3]))


def attend_forward(query_pos, key_pos, value_pos):
    factor = HD ** (-0.5)
    scores = (
        jnp.einsum(
            "fphe,gphe->phfg",
            to_heads(query_pos),
            to_heads(key_pos),
            preferred_element_type=jnp.float32,
        )
        * factor
    )
    weights = jnp.exp(scores)
    probs = weights / jnp.sum(weights, axis=-1, keepdims=True)
    probs_b = probs.astype(jnp.bfloat16)
    attended = jnp.einsum(
        "phfg,gphe->fphe", probs_b, to_heads(value_pos), preferred_element_type=jnp.float32
    )
    return (probs, probs_b, from_heads(attended.astype(jnp.bfloat16)))


def attend_backward(probs, probs_b, query_pos, key_pos, value_pos, grad_pos):
    factor = HD ** (-0.5)
    grad_h = to_heads(grad_pos)
    dprobs = jnp.einsum(
        "fphe,gphe->phfg", grad_h, to_heads(value_pos), preferred_element_type=jnp.float32
    )
    delta = jnp.sum(probs * dprobs, axis=-1, keepdims=True)
    dscores = (probs * (dprobs - delta)).astype(jnp.bfloat16)
    dnormq = (
        jnp.einsum(
            "phfg,gphe->fphe", dscores, to_heads(key_pos), preferred_element_type=jnp.float32
        )
        * factor
    )
    dnormk = (
        jnp.einsum(
            "phfg,fphe->gphe", dscores, to_heads(query_pos), preferred_element_type=jnp.float32
        )
        * factor
    )
    dvalue = jnp.einsum("phfg,fphe->gphe", probs_b, grad_h, preferred_element_type=jnp.float32)
    return (
        from_heads(dnormq.astype(jnp.bfloat16)),
        from_heads(dnormk.astype(jnp.bfloat16)),
        from_heads(dvalue.astype(jnp.bfloat16)),
    )


def make_block(feats, cots, dquery, dkey, dvalue, attended):

    def block(start, count):
        return jnp.concatenate(
            [
                contract_rows(feats, dquery),
                contract_rows(feats, dkey),
                contract_rows(feats, dvalue),
                contract_rows(cots, attended),
            ],
            axis=1,
        )

    return block


def on_device(frames_in, w_query, w_key, w_value, w_out, grad_in):
    full_q, full_k, full_v, full_o = (
        lax.all_gather(w_query, ("dp", "seq"), axis=0, tiled=True),
        lax.all_gather(w_key, ("dp", "seq"), axis=0, tiled=True),
        lax.all_gather(w_value, ("dp", "seq"), axis=0, tiled=True),
        lax.all_gather(w_out, ("dp", "seq"), axis=1, tiled=True),
    )
    lead = frames_in.shape
    width = full_q.shape[1]
    model = lead[3]
    flat = frames_in.reshape(-1, model)
    upstream = grad_in.reshape(-1, model)
    tok_shape = lead[:3] + (width,)
    query = jnp.dot(flat, full_q, preferred_element_type=jnp.float32)
    key_raw = jnp.dot(flat, full_k, preferred_element_type=jnp.float32)
    value_raw = jnp.dot(flat, full_v, preferred_element_type=jnp.float32)
    normq = norm_heads(query).astype(jnp.bfloat16).reshape(tok_shape)
    normk = norm_heads(key_raw).astype(jnp.bfloat16).reshape(tok_shape)
    value_b = value_raw.astype(jnp.bfloat16).reshape(tok_shape)
    grad_att = contract_cols(upstream, full_o).astype(jnp.bfloat16).reshape(tok_shape)
    query_pos, key_pos, value_pos = (
        lax.all_to_all(normq, "seq", split_axis=2, concat_axis=1, tiled=True),
        lax.all_to_all(normk, "seq", split_axis=2, concat_axis=1, tiled=True),
        lax.all_to_all(value_b, "seq", split_axis=2, concat_axis=1, tiled=True),
    )
    grad_pos = lax.all_to_all(grad_att, "seq", split_axis=2, concat_axis=1, tiled=True)
    probs, probs_b, attended_pos = attend_forward(query_pos, key_pos, value_pos)
    attended_tok = lax.all_to_all(attended_pos, "seq", split_axis=1, concat_axis=2, tiled=True)
    dnormq_pos, dnormk_pos, dvalue_pos = attend_backward(
        probs, probs_b, query_pos, key_pos, value_pos, grad_pos
    )
    dnormq, dnormk, dvalue = (
        lax.all_to_all(dnormq_pos, "seq", split_axis=1, concat_axis=2, tiled=True),
        lax.all_to_all(dnormk_pos, "seq", split_axis=1, concat_axis=2, tiled=True),
        lax.all_to_all(dvalue_pos, "seq", split_axis=1, concat_axis=2, tiled=True),
    )
    back_q = jax.vjp(norm_heads, query)[1]
    back_k = jax.vjp(norm_heads, key_raw)[1]
    dquery = back_q(dnormq.reshape(-1, width).astype(jnp.float32))[0].astype(jnp.bfloat16)
    dkey = back_k(dnormk.reshape(-1, width).astype(jnp.float32))[0].astype(jnp.bfloat16)
    dvalue_flat = dvalue.reshape(-1, width)
    attended_flat = attended_tok.reshape(-1, width)
    term_x = (
        contract_cols(dquery, full_q)
        + contract_cols(dkey, full_k)
        + contract_cols(dvalue_flat, full_v)
    )
    grad_frames = lax.psum_scatter(
        term_x.reshape(lead).astype(jnp.bfloat16), "heads", scatter_dimension=3, tiled=True
    )
    rows = w_query.shape[0]
    tokens_all = flat.shape[0] * lax.axis_size("dp") * lax.axis_size("seq")
    gscale = tokens_all ** (-0.5)
    block = make_block(flat, upstream, dquery, dkey, dvalue_flat, attended_flat)
    sums = lax.psum_scatter(
        block(jnp.int32(0), lax.axis_size(("dp", "seq")) * rows),
        ("dp", "seq"),
        scatter_dimension=0,
        tiled=True,
    )
    sums = sums * gscale
    grad_query = sums[:, :width].astype(jnp.bfloat16)
    grad_key = sums[:, width : 2 * width].astype(jnp.bfloat16)
    grad_value = sums[:, 2 * width : 3 * width].astype(jnp.bfloat16)
    grad_out = sums[:, 3 * width :].T.astype(jnp.bfloat16)
    return (grad_frames, grad_query, grad_key, grad_value, grad_out)


def solution(mesh):
    placed = (
        P("dp", "seq", None, None),
        P(("dp", "seq"), "heads"),
        P(("dp", "seq"), "heads"),
        P(("dp", "seq"), "heads"),
        P("heads", ("dp", "seq")),
        P("dp", "seq", None, None),
    )
    return jax.shard_map(
        on_device,
        mesh=mesh,
        in_specs=placed,
        out_specs=(
            P("dp", "seq", None, "heads"),
            P(("dp", "seq"), "heads"),
            P(("dp", "seq"), "heads"),
            P(("dp", "seq"), "heads"),
            P("heads", ("dp", "seq")),
        ),
        check_vma=False,
    )
```

profile of v0, /device:TPU:1, one launch (start us, length us, event | category | flops | bytes accessed | tf_op | source)
XLA Modules:
  0.0 1034.1 jit_solution(14810025684920081759)
XLA Ops:
  10.0 109.9 %all-gather.9.cloned.1.call-done = bf16[512,2048]{0,1:T(8,128)(2,1)} async-done(((bf16[512,32]{0,1:T(8,128)(2,1)}), bf16[512,2048]{0,1:T(8,128)(2,1)}) %all-gather.9.cloned.1.call-update) | async-done | bytes 2097168 | tf_op jit(solution)/shard_map/all_gather | solution.py:107
  119.9 3.5 fusion.24
  124.7 4.6 reduce.8
  131.5 5.4 all-to-all-start.2
  136.9 92.3 %all-gather.11.cloned.1.call-done = bf16[2048,512]{1,0:T(8,128)(2,1)} async-done(((bf16[32,512]{1,0:T(8,128)(2,1)}), bf16[2048,512]{1,0:T(8,128)(2,1)}) %all-gather.11.cloned.1.call-update) | async-done | bytes 2097168 | tf_op jit(solution)/shard_map/all_gather | solution.py:106
  229.2 2.8 fusion.27
  232.9 4.6 reduce.11
  239.7 5.1 all-to-all-start.3
  244.8 93.1 %all-gather.5.cloned.1.call-done = bf16[2048,512]{1,0:T(8,128)(2,1)} async-done(((bf16[32,512]{1,0:T(8,128)(2,1)}), bf16[2048,512]{1,0:T(8,128)(2,1)}) %all-gather.5.cloned.1.call-update) | async-done | bytes 2097168 | tf_op jit(solution)/shard_map/all_gather | solution.py:105
  337.9 4.0 copy.77
  341.9 2.9 multiply_reduce_fusion.4
  345.7 3.5 copy.78
  349.3 5.6 reduce.9
  357.1 6.3 all-to-all-start
  363.4 85.0 %all-gather.7.cloned.1.call-done = bf16[2048,512]{1,0:T(8,128)(2,1)} async-done(((bf16[32,512]{1,0:T(8,128)(2,1)}), bf16[2048,512]{1,0:T(8,128)(2,1)}) %all-gather.7.cloned.1.call-update) | async-done | bytes 2097168 | tf_op jit(solution)/shard_map/all_gather | solution.py:104
  448.4 4.0 copy.79
  452.4 2.9 multiply_reduce_fusion.3
  457.2 3.6 copy.80
  460.7 5.6 reduce.10
  468.5 5.5 all-to-all-start.1
  474.0 4.4 reshape.201
  478.4 5.1 bitcast_reduce_fusion
  485.5 4.4 reshape.199
  489.9 5.1 bitcast_reduce_fusion.1
  497.0 4.6 reshape.195
  501.6 5.1 bitcast_reduce_fusion.3
  508.7 4.4 reshape.197
  513.1 5.1 bitcast_reduce_fusion.2
  530.1 8.0 all-to-all-start.4
  542.9 4.9 all-to-all-done.4
  547.8 6.1 all-to-all-start.5
  553.9 3.2 fusion.30
  561.3 3.1 fusion.31
  568.5 2.4 reshape.185
  570.9 2.6 copy.91
  573.5 7.8 all-to-all-start.6
  583.0 2.4 reshape.186
  585.4 2.5 copy.96
  590.9 7.8 all-to-all-start.7
  598.8 4.3 convolution_bitcast_fusion.1
  604.1 3.3 convolution_bitcast_fusion.3
  607.4 3.3 convolution_bitcast_fusion.2
  610.7 3.2 convolution_bitcast_fusion
  613.9 10.0 pad_maximum_fusion
  623.8 17.7 %copy.111 = f32[2048,2048]{1,0:T(8,128)} copy(f32[2048,2048]{0,1:T(8,128)} %pad_maximum_fusion) | data formatting | bytes 33554432
  646.4 3.8 fusion
  650.2 327.5 %reduce-scatter.7.cloned.1.call-done = f32[32,2048]{1,0:T(8,128)} async-done(((f32[2048,2048]{1,0:T(8,128)}), f32[32,2048]{1,0:T(8,128)}) %reduce-scatter.7.cloned.1.call-update) | async-done | bytes 262160
  982.0 44.8 %reduce-scatter.5.cloned.1.call-done = bf16[1,1,512,512]{3,2,1,0:T(8,128)(2,1)} async-done(((bf16[1,1,512,2048]{3,2,1,0:T(8,128)(2,1)}), bf16[1,1,512,512]{3,2,1,0:T(8,128)(2,1)}) %reduce-scatter.5.cloned.1.call-update) | async-done | bytes 524304 | tf_op jit(solution)/shard_map/reduce_scatter | solution.py:149
  (99 shorter events, 62.2 us)
Async XLA Ops:
  7.2 222.0 %copy-start = (bf16[1,1,512,2048]{3,2,1,0:T(8,128)(2,1)S(1)}, bf16[1,1,512,2048]{3,2,1,0:T(8,128)(2,1)}, u32[]{:S(2)}) copy-start(bf16[1,1,512,2048]{3,2,1,0:T(8,128)(2,1)} %param.6) | copy-start | bytes 6291460
  7.2 112.7 %all-gather.9.cloned.1.call-start = ((), (), s32[]{:S(2)}) async-start(), calls=%async_computation.12 | async-start | bytes 2129920 | tf_op jit(solution)/shard_map/all_gather | solution.py:107
  7.9 221.3 %all-gather.11.cloned.1.call-start = ((), (), s32[]{:S(2)}) async-start(), calls=%async_computation.13 | async-start | bytes 2129920 | tf_op jit(solution)/shard_map/all_gather | solution.py:106
  8.7 329.3 %all-gather.5.cloned.1.call-start = ((), (), s32[]{:S(2)}) async-start(), calls=%async_computation.10 | async-start | bytes 2129920 | tf_op jit(solution)/shard_map/all_gather | solution.py:105
  9.4 439.0 %all-gather.7.cloned.1.call-start = ((), (), s32[]{:S(2)}) async-start(), calls=%async_computation.11 | async-start | bytes 2129920 | tf_op jit(solution)/shard_map/all_gather | solution.py:104
  131.5 108.2 %all-to-all-start.2 = ((bf16[32,2,4096]{2,1,0:T(2,128)(2,1)}), bf16[32,2,4096]{2,1,0:T(2,128)(2,1)}, u32[]{:S(2)}, u32[]{:S(2)}) async-start(bf16[32,2,4096]{2,1,0:T(2,128)(2,1)} %reshape.200), calls=%async_computation.2 | async-start | bytes 1048576 | tf_op jit(solution)/shard_map/all_to_all | solution.py:127
  239.7 117.3 %all-to-all-start.3 = ((bf16[32,2,4096]{2,1,0:T(2,128)(2,1)}), bf16[32,2,4096]{2,1,0:T(2,128)(2,1)}, u32[]{:S(2)}, u32[]{:S(2)}) async-start(bf16[32,2,4096]{2,1,0:T(2,128)(2,1)} %reshape.198), calls=%async_computation.3 | async-start | bytes 1048576 | tf_op jit(solution)/shard_map/all_to_all | solution.py:125
  357.1 111.4 %all-to-all-start = ((bf16[32,2,4096]{2,1,0:T(2,128)(2,1)}), bf16[32,2,4096]{2,1,0:T(2,128)(2,1)}, u32[]{:S(2)}, u32[]{:S(2)}) async-start(bf16[32,2,4096]{2,1,0:T(2,128)(2,1)} %reshape.194), calls=%async_computation | async-start | bytes 1048576 | tf_op jit(solution)/shard_map/all_to_all | solution.py:124
  455.3 1.0 copy-start.3
  468.5 40.2 %all-to-all-start.1 = ((bf16[32,2,4096]{2,1,0:T(2,128)(2,1)}), bf16[32,2,4096]{2,1,0:T(2,128)(2,1)}, u32[]{:S(2)}, u32[]{:S(2)}) async-start(bf16[32,2,4096]{2,1,0:T(2,128)(2,1)} %reshape.196), calls=%async_computation.1 | async-start | bytes 1048576 | tf_op jit(solution)/shard_map/all_to_all | solution.py:123
  520.2 2.1 copy-start.14
  520.2 2.1 copy-start.15
  523.2 2.3 copy-start.17
  525.7 0.8 copy-start.13
  530.1 17.7 %all-to-all-start.4 = ((bf16[1,32,16,512]{3,2,0,1:T(8,128)(2,1)}), bf16[1,32,16,512]{3,2,0,1:T(8,128)(2,1)}, u32[]{:S(2)}, u32[]{:S(2)}) async-start(bf16[1,32,16,512]{3,2,0,1:T(8,128)(2,1)} %bitcast.131), calls=%async_computation.4 | async-start | bytes 1048576 | tf_op jit(solution)/shard_map/all_to_all | solution.py:134
  547.8 25.7 %all-to-all-start.5 = ((bf16[1,32,16,512]{3,2,0,1:T(8,128)(2,1)}), bf16[1,32,16,512]{3,2,0,1:T(8,128)(2,1)}, u32[]{:S(2)}, u32[]{:S(2)}) async-start(bf16[1,32,16,512]{3,2,0,1:T(8,128)(2,1)} %bitcast.130), calls=%async_computation.5 | async-start | bytes 1048576 | tf_op jit(solution)/shard_map/all_to_all | solution.py:135
  573.5 17.4 %all-to-all-start.6 = ((bf16[1,32,16,512]{3,2,0,1:T(8,128)(2,1)}), bf16[1,32,16,512]{3,2,0,1:T(8,128)(2,1)}, u32[]{:S(2)}, u32[]{:S(2)}) async-start(bf16[1,32,16,512]{3,2,0,1:T(8,128)(2,1)} %bitcast.129), calls=%async_computation.6 | async-start | bytes 1048576 | tf_op jit(solution)/shard_map/all_to_all | solution.py:136
  588.0 1.6 copy-start.4
  588.0 1.9 copy-start.6
  590.9 19.8 %all-to-all-start.7 = ((bf16[1,32,16,512]{3,2,0,1:T(8,128)(2,1)}), bf16[1,32,16,512]{3,2,0,1:T(8,128)(2,1)}, u32[]{:S(2)}, u32[]{:S(2)}) async-start(bf16[1,32,16,512]{3,2,0,1:T(8,128)(2,1)} %bitcast.128), calls=%async_computation.8 | async-start | bytes 1048576 | tf_op jit(solution)/shard_map/all_to_all | solution.py:129
  598.7 379.0 %reduce-scatter.7.cloned.1.call-start = ((), (), s32[]{:S(2)}) async-start(), calls=%async_computation.15 | async-start | bytes 17039360
  598.7 4.4 copy-start.5
  603.1 1.0 copy-start.9
  603.4 4.0 copy-start.11
  610.7 3.2 copy-start.2
  641.5 1.6 copy-start.7
  641.5 1.7 copy-start.12
  641.5 3.0 copy-start.10
  641.5 385.2 %reduce-scatter.5.cloned.1.call-start = ((), (), s32[]{:S(2)}) async-start(), calls=%async_computation.14 | async-start | bytes 2621440 | tf_op jit(solution)/shard_map/reduce_scatter | solution.py:149
  643.2 1.6 copy-start.8
  644.8 1.6 copy-start.16
  650.2 376.6 %copy-start.1 = (bf16[1,1,512,2048]{3,2,1,0:T(8,128)(2,1)S(1)}, bf16[1,1,512,2048]{3,2,1,0:T(8,128)(2,1)}, u32[]{:S(2)}) copy-start(bf16[1,1,512,2048]{3,2,1,0:T(8,128)(2,1)} %param.6) | copy-start | bytes 6291460
Sparse Core Ops, SparseCore 0:
  9.9 109.9 all-gather.8
  121.7 107.4 all-gather.10
  231.1 106.8 all-gather.4
  339.7 108.7 all-gather.6
  641.6 336.0 reduce-scatter.6
  980.7 46.0 reduce-scatter.4
where the time goes:
time: 1050 us; the launch traced here: 1030 us
  waiting for transfers between devices  760 us (72%)
  local copies, waits for them, and re-layouts  123 us (12%)
  starting transfers between devices  52.4 us (5%)
  matrix products  43.9 us (4%)
  other arithmetic  39.5 us (4%)
  between operations  14.9 us (1%)
    unnamed x7, waiting for transfers between devices  330 us
    all_gather x1, waiting for transfers between devices, on_device(): lax.all_gather(w_out, ('dp', 'seq'), axis=1, tiled=True)  110 us
    all_gather x1, waiting for transfers between devices, on_device(): lax.all_gather(w_key, ('dp', 'seq'), axis=0, tiled=True)  93.1 us
    all_gather x1, waiting for transfers between devices, on_device(): lax.all_gather(w_value, ('dp', 'seq'), axis=0, tiled=True)  92.3 us
    all_gather x1, waiting for transfers between devices, on_device(): lax.all_gather(w_query, ('dp', 'seq'), axis=0, tiled=True)  85 us
    unnamed x51, local copies, waits for them, and re-layouts  53.7 us
    reduce_scatter x1, waiting for transfers between devices, on_device(): lax.psum_scatter(term_x.reshape(lead).astype(jnp.bfloat16), 'heads', scat...  44.8 us
  transfers between devices with their start and end apart: 14, of which 7 were waited for; matrix products, arithmetic and copies ran while one was open for 15% of the time, Pallas kernels for 0%

commit v1 on v0

v1 whole, which is shorter than its diff:
```python
import functools

import jax
import jax.numpy as jnp
from jax import lax
from jax.experimental import pallas as pl
from jax.experimental.pallas import tpu as pltpu
from jax.sharding import Mesh
from jax.sharding import PartitionSpec as P

HD = 128
EPS = 1e-06
FACTOR = HD ** (-0.5)
SEQ = ("y", "z", "x")
OFFSETS = (0, -1, 1, 2)
BF16 = jnp.bfloat16
F32 = jnp.float32
VMEM = pl.BlockSpec(memory_space=pltpu.VMEM)
ANY = pl.BlockSpec(memory_space=pl.ANY)
LIMIT = 60 * 1024 * 1024


def dot(left, right, dims):
    return lax.dot_general(left, right, (dims, ((), ())), preferred_element_type=F32)


def normed(t):
    scale = lax.rsqrt(jnp.mean(t * t, axis=-1, keepdims=True) + EPS)
    return t * scale, scale


def norm_back(n, scale, grad):
    return scale * (grad - n * jnp.mean(n * grad, axis=-1, keepdims=True))


def attention(q, k, v, g, same):
    nq, rq = normed(q)
    nk, rk = normed(k)
    nqb, nkb, vb, gb = nq.astype(BF16), nk.astype(BF16), v.astype(BF16), g.astype(BF16)
    scores = dot(nqb, nkb, ((1,), (1,))) * FACTOR
    weights = jnp.where(same, jnp.exp(scores), 0.0)
    probs = weights / jnp.sum(weights, axis=-1, keepdims=True)
    probs_b = probs.astype(BF16)
    att = dot(probs_b, vb, ((1,), (0,)))
    dprobs = dot(gb, vb, ((1,), (1,)))
    weighted = probs * dprobs
    delta = jnp.sum(weighted, axis=-1, keepdims=True)
    dscores = (weighted - probs * delta).astype(BF16)
    dnq = dot(dscores, nkb, ((1,), (0,))) * FACTOR
    dnk = dot(dscores, nqb, ((0,), (0,))) * FACTOR
    dv = dot(probs_b, gb, ((0,), (0,)))
    return norm_back(nq, rq, dnq), norm_back(nk, rk, dnk), dv, att


def main_kernel(place, x0, x1, u0, u1, *refs):
    pieces, (t0, t1, d0, d1), (w, proj, back, sems) = refs[:10], refs[10:14], refs[14:]
    y, x = place[0], place[1]
    copies = []

    def fetch(src, dst):
        copies.append(pltpu.make_async_copy(src, dst, sems.at[len(copies)]))
        copies[-1].start()

    for half in range(2):
        own, before, after, far_a, far_b = pieces[5 * half : 5 * half + 5]
        for i, outer in enumerate(OFFSETS):
            for j, inner in enumerate(OFFSETS):
                if i < 3:
                    src = (own, before, after)[i].at[j]
                else:
                    src = (far_a if j < 2 else far_b).at[j % 2]
                yy, xx = (inner, outer) if half == 0 else (outer, inner)
                fetch(src, w.at[half, lax.rem(y + yy + 4, 4), :, lax.rem(x + xx + 4, 4)])
    for copy in copies:
        copy.wait()

    row = lax.broadcasted_iota(jnp.int32, (256, 256), 0)
    col = lax.broadcasted_iota(jnp.int32, (256, 256), 1)
    same = lax.rem(row, 8) == lax.rem(col, 8)
    for x_in, u_in, t_out, d_out in ((x0, u0, t0, d0), (x1, u1, t1, d1)):
        for kind in range(4):
            tokens = (u_in if kind == 3 else x_in)[...].reshape(512, 2048)
            cols = slice(kind * 256, kind * 256 + 256)
            acc = dot(tokens[:, :1024], w[0, :, :, :, :, cols].reshape(1024, 256), ((1,), (0,)))
            acc += dot(tokens[:, 1024:], w[1, :, :, :, :, cols].reshape(1024, 256), ((1,), (0,)))
            proj[:, :, :, cols] = acc.reshape(32, 2, 8, 256)
        for head in range(2):
            for part in range(2):
                at = [kind * 256 + head * 128 for kind in range(4)]
                out = attention(*(proj[:, part, :, a : a + 128].reshape(256, 128) for a in at), same)
                for a, value in zip(at, out):
                    back[:, part, :, a : a + 128] = value.reshape(32, 8, 128)
        d_all = back[...].reshape(512, 1024).astype(BF16)
        d_out[...] = d_all
        for chunk in range(4):
            half, first = chunk // 2, 2 * (chunk % 2)
            rows = w[half, first : first + 2, :, :, :, :768].reshape(512, 768)
            t_out[chunk] = dot(d_all[:, :768], rows, ((1,), (1,))).astype(BF16)


def grads_kernel(x0, x1, u0, u1, d0, d1, out):
    for block in range(8):
        half, s = block // 4, 8 * (block % 4)
        cols = slice(block * 256, block * 256 + 256)
        for a, b, lo, hi in ((x0, x1, 0, 768), (u0, u1, 768, 1024)):
            acc = dot(a[:, :, cols].reshape(512, 256), d0[:, lo:hi], ((0,), (0,)))
            acc += dot(b[:, :, cols].reshape(512, 256), d1[:, lo:hi], ((0,), (0,)))
            out[s : s + 8, half, :, lo:hi] = acc.reshape(8, 32, hi - lo).astype(BF16)


def shift(t, axis, by):
    n = lax.axis_size(axis)
    return lax.ppermute(t, axis, [(i, (i + by) % n) for i in range(n)])


def ring(t, axis):
    before, after = shift(t, axis, 1), shift(t, axis, -1)
    half = t.shape[0] // 2
    return t, before, after, shift(before[:half], axis, 1), shift(after[half:], axis, -1)


def stacked(blocks):
    own, before, after, far_a, far_b = blocks
    return jnp.stack([own, before, after, jnp.concatenate([far_a, far_b], axis=0)])


def exchange(t, axis):
    return lax.all_to_all(t, axis, 0, 0, tiled=True)


def gathered(w_query, w_key, w_value, w_out):
    w = jnp.stack([w_query, w_key, w_value, w_out.T], axis=1)
    w = w.reshape(32, 4, 2, 256).transpose(2, 0, 1, 3).reshape(2, 32, 1024)
    w = exchange(w, "dp")
    other = shift(w, "z", 1)
    low = lax.axis_index("z") == 0
    pair = jnp.stack([jnp.where(low, w, other), jnp.where(low, other, w)], axis=1)
    first = ring(stacked(ring(pair[0], "y")), "x")
    second = ring(stacked(ring(pair[1], "x")), "y")
    return first + second


def on_device(frames_in, w_query, w_key, w_value, w_out, grad_in):
    x0 = exchange(frames_in.reshape(32, 16, 2048), SEQ)
    u0 = exchange(grad_in.reshape(32, 16, 2048), SEQ)
    pieces = gathered(w_query, w_key, w_value, w_out)
    x1 = shift(x0, "dp", 1)
    u1 = shift(u0, "dp", 1)
    place = jnp.stack([lax.axis_index("y"), lax.axis_index("x")]).astype(jnp.int32)
    t0, t1, d0, d1 = pl.pallas_call(
        main_kernel,
        out_shape=[jax.ShapeDtypeStruct((4, 512, 512), BF16)] * 2
        + [jax.ShapeDtypeStruct((512, 1024), BF16)] * 2,
        in_specs=[pl.BlockSpec(memory_space=pltpu.SMEM)] + [VMEM] * 4 + [ANY] * 10,
        out_specs=[VMEM] * 4,
        scratch_shapes=[
            pltpu.VMEM((2, 4, 2, 4, 32, 1024), BF16),
            pltpu.VMEM((32, 2, 8, 1024), F32),
            pltpu.VMEM((32, 2, 8, 1024), F32),
            pltpu.SemaphoreType.DMA((32,)),
        ],
        compiler_params=pltpu.CompilerParams(vmem_limit_bytes=LIMIT),
        cost_estimate=pl.CostEstimate(flops=9_000_000_000, bytes_accessed=18 << 20, transcendentals=1 << 19),
    )(place, x0, x1, u0, u1, *pieces)
    term = t0.astype(F32) + shift(t1, "dp", 1).astype(F32)
    mine = lax.psum_scatter(term.astype(BF16), "heads", scatter_dimension=0, tiled=True)
    grad_frames = exchange(mine.reshape(32, 16, 512), SEQ).reshape(1, 1, 512, 512)
    grads = pl.pallas_call(
        grads_kernel,
        out_shape=jax.ShapeDtypeStruct((32, 2, 32, 1024), BF16),
        in_specs=[VMEM] * 6,
        out_specs=VMEM,
        compiler_params=pltpu.CompilerParams(vmem_limit_bytes=LIMIT),
        cost_estimate=pl.CostEstimate(flops=4_300_000_000, bytes_accessed=14 << 20, transcendentals=0),
    )(x0, x1, u0, u1, d0, d1)
    gscale = 32768 ** (-0.5)
    sums = jnp.sum(exchange(grads, SEQ).astype(F32), axis=0) * gscale
    sums = exchange(sums.astype(BF16), "dp").reshape(2, 32, 4, 256)
    gq, gk, gv, go = (
        jnp.concatenate([sums[0, :, kind], sums[1, :, kind]], axis=1) for kind in range(4)
    )
    return grad_frames, gq, gk, gv, go.T


def solution(mesh):
    fine = Mesh(mesh.devices.reshape(2, 4, 2, 4, 4), ("dp", "y", "z", "x", "heads"))
    tokens = P("dp", SEQ, None, None)
    rows = P(("dp",) + SEQ, "heads")
    cols = P("heads", ("dp",) + SEQ)
    return jax.shard_map(
        on_device,
        mesh=fine,
        in_specs=(tokens, rows, rows, rows, cols, tokens),
        out_specs=(P("dp", SEQ, None, "heads"), rows, rows, rows, cols),
        check_vma=False,
    )
```

time: 1050 us -> 328 us (0.31); the launches traced: 1030 us -> 326 us
  waiting for transfers between devices: 760 us -> 168 us
  local copies, waits for them, and re-layouts: 123 us -> 6.71 us
  blocking collectives: 0 us -> 46.3 us
  matrix products: 43.9 us -> 0 us
  Pallas kernels: 0 us -> 30.2 us
  other arithmetic: 39.5 us -> 10.3 us
    all_gather x4 -> x0, waiting for transfers between devices: 380 us -> none  [the longest x1 110 us: on_device(): lax.all_gather(w_out, ('dp', 'seq'), axis=1, tiled=True)]
    unnamed x7 -> x1, waiting for transfers between devices: 330 us -> 0.02 us
    all_to_all x8 -> x3, waiting for transfers between devices: 4.96 us -> 75.8 us  [exchange(): return lax.all_to_all(t, axis, 0, 0, tiled=True)]
    unnamed x51 -> x21, local copies, waits for them, and re-layouts: 53.7 us -> 1.53 us
    all_to_all x0 -> x3, blocking collectives: none -> 46.3 us  [exchange(): return lax.all_to_all(t, axis, 0, 0, tiled=True)]
    dot_general x17 -> x0, matrix products: 43.9 us -> none  [the longest x4 14 us: contract_rows(): lax.dot_general(left, right, (((0,), (0,)), ((), ())), preferred_element_...]
    ppermute x0 -> x20, waiting for transfers between devices: none -> 42 us  [shift(): return lax.ppermute(t, axis, [(i, (i + by) % n) for i in range(n)])]
    all_to_all x8 -> x3, starting transfers between devices: 52 us -> 21 us  [exchange(): return lax.all_to_all(t, axis, 0, 0, tiled=True)]
  transfers between devices with their start and end apart: 14 -> 24, of which waited for: 7 -> 15; matrix products, arithmetic and copies ran while one was open for 15% -> 1% of each run, Pallas kernels for 0% -> 3%
where the time goes in v1:
time: 328 us; the launch traced here: 326 us
  waiting for transfers between devices  168 us (51%)
  starting transfers between devices  49.5 us (15%)
  blocking collectives  46.3 us (14%)
  Pallas kernels  30.2 us (9%)
  between operations  14.3 us (4%)
  other arithmetic  10.3 us (3%)
  local copies, waits for them, and re-layouts  6.71 us (2%)
    all_to_all x3, waiting for transfers between devices, exchange(): return lax.all_to_all(t, axis, 0, 0, tiled=True)  75.8 us
    reduce_scatter x1, waiting for transfers between devices, on_device(): lax.psum_scatter(term.astype(BF16), 'heads', scatter_dimension=0, tiled=T...  50.5 us
    all_to_all x3, blocking collectives, exchange(): return lax.all_to_all(t, axis, 0, 0, tiled=True)  46.3 us
    ppermute x20, waiting for transfers between devices, shift(): return lax.ppermute(t, axis, [(i, (i + by) % n) for i in range(n)])  42 us
    ppermute x20, starting transfers between devices, shift(): return lax.ppermute(t, axis, [(i, (i + by) % n) for i in range(n)])  28.5 us
    all_to_all x3, starting transfers between devices, exchange(): return lax.all_to_all(t, axis, 0, 0, tiled=True)  21 us
    pallas_call x1, Pallas kernels, on_device(): pl.pallas_call(main_kernel, out_shape=[jax.ShapeDtypeStruct((4, 512, 512)...  19.7 us
    pallas_call x1, Pallas kernels, on_device(): pl.pallas_call(grads_kernel, out_shape=jax.ShapeDtypeStruct((32, 2, 32, 1...  10.5 us
  transfers between devices with their start and end apart: 24, of which 15 were waited for; matrix products, arithmetic and copies ran while one was open for 1% of the time, Pallas kernels for 3%

profile of v1, /device:TPU:1, one launch (start us, length us, event | category | flops | bytes accessed | tf_op | source)
XLA Modules:
  0.0 325.6 jit_solution(11762639338816634613)
XLA Ops:
  7.2 0.8 stack.60
  8.0 0.8 stack.61
  8.8 0.8 stack.62
  9.7 0.8 stack.63
  10.9 6.7 %all_to_all.30 = bf16[2,32,1024]{2,1,0:T(8,128)(2,1)S(1)} all-to-all(bf16[2,32,1024]{2,1,0:T(8,128)(2,1)S(1)} %reshape.39), channel_id=1, replica_groups=mesh['dp'=2,'y'=4,'z'=2,'x'=4,'heads'=4] {'dp'}, dimensions={0} | all-to-all | bytes 262144 | tf_op jit(solution)/shard_map/all_to_all | solution.py:128
  17.6 33.5 %all_to_all.31.u0 = bf16[32,16,2048]{2,1,0:T(8,128)(2,1)S(1)} all-to-all(bf16[32,16,2048]{2,1,0:T(8,128)(2,1)} %bitcast.43), channel_id=1, replica_groups=mesh['dp'=2,'y'=4,'z'=2,'x'=4,'heads'=4] {'y','z','x'}, dimensions={0} | all-to-all | bytes 4194304 | tf_op jit(solution)/shard_map/all_to_all | solution.py:128
  51.1 6.3 %all-to-all-start = ((bf16[32,16,2048]{2,1,0:T(8,128)(2,1)}), bf16[32,16,2048]{2,1,0:T(8,128)(2,1)}, u32[]{:S(2)}, u32[]{:S(2)}) async-start(bf16[32,16,2048]{2,1,0:T(8,128)(2,1)} %bitcast.2), calls=%async_computation | async-start | bytes 4194304 | tf_op jit(solution)/shard_map/all_to_all | solution.py:128
  57.4 1.2 collective-permute-start.2
  58.7 1.7 collective-permute-start.1
  60.4 23.9 %all-to-all-done.x0 = bf16[32,16,2048]{2,1,0:T(8,128)(2,1)} async-done(((bf16[32,16,2048]{2,1,0:T(8,128)(2,1)}), bf16[32,16,2048]{2,1,0:T(8,128)(2,1)}, u32[]{:S(2)}, u32[]{:S(2)}) %all-to-all-start) | async-done | bytes 2097184 | tf_op jit(solution)/shard_map/all_to_all | solution.py:128
  84.2 3.8 %collective-permute-start = (bf16[32,16,2048]{2,1,0:T(8,128)(2,1)}, bf16[32,16,2048]{2,1,0:T(8,128)(2,1)}, u32[]{:S(2)}, u32[]{:S(2)}) collective-permute-start(bf16[32,16,2048]{2,1,0:T(8,128)(2,1)} %all-to-all-done.x0), channel_id=1, source_target_pairs={{0,128},{128,0},{1,129},{129,1},{2,130},{130,2},{3,131},{131,3},{4... | collective-permute-start | bytes 6291464 | tf_op jit(solution)/shard_map/ppermute | solution.py:113
  88.5 1.2 collective-permute-start.11
  89.6 3.7 %collective-permute-done.12 = bf16[2,32,1024]{2,1,0:T(8,128)(2,1)S(1)} collective-permute-done((bf16[2,32,1024]{2,1,0:T(8,128)(2,1)S(1)}, bf16[2,32,1024]{2,1,0:T(8,128)(2,1)S(1)}, u32[]{:S(2)}, u32[]{:S(2)}) %collective-permute-start.12) | collective-permute-done | bytes 131104 | tf_op jit(solution)/shard_map/ppermute | solution.py:113
  93.3 1.0 collective-permute-start.14
  94.9 1.6 collective-permute-done.14
  96.4 2.3 collective-permute-done.13
  98.8 3.5 %collective-permute-start.16 = (bf16[4,2,32,1024]{3,2,1,0:T(8,128)(2,1)S(1)}, bf16[4,2,32,1024]{3,2,1,0:T(8,128)(2,1)S(1)}, u32[]{:S(2)}, u32[]{:S(2)}) collective-permute-start(bf16[4,2,32,1024]{3,2,1,0:T(8,128)(2,1)S(1)} %pad_maximum_fusion.1.refs_5_), channel_id=1, source_target_pairs={{0,96},{32,0},{64,32},{96,64},{1,97},{33,1},{65,33},{97,65},{2,98}... | collective-permute-start | bytes 1572872 | tf_op jit(solution)/shard_map/ppermute | solution.py:113
  102.4 1.4 collective-permute-start.3
  103.7 11.3 %collective-permute-done.4 = bf16[2,32,1024]{2,1,0:T(8,128)(2,1)S(1)} collective-permute-done((bf16[2,32,1024]{2,1,0:T(8,128)(2,1)S(1)}, bf16[2,32,1024]{2,1,0:T(8,128)(2,1)S(1)}, u32[]{:S(2)}, u32[]{:S(2)}) %collective-permute-start.4) | collective-permute-done | bytes 131104 | tf_op jit(solution)/shard_map/ppermute | solution.py:113
  115.1 2.2 collective-permute-start.6
  117.4 1.2 collective-permute-done.6
  118.6 0.8 collective-permute-start.15
  119.4 2.3 collective-permute-done.5
  122.3 1.3 collective-permute-start.7
  123.5 7.2 %collective-permute-done.15.refs_6_ = bf16[4,2,32,1024]{3,2,1,0:T(8,128)(2,1)S(1)} collective-permute-done((bf16[4,2,32,1024]{3,2,1,0:T(8,128)(2,1)S(1)}, bf16[4,2,32,1024]{3,2,1,0:T(8,128)(2,1)S(1)}, u32[]{:S(2)}, u32[]{:S(2)}) %collective-permute-start.15) | collective-permute-done | bytes 524320 | tf_op jit(solution)/shard_map/ppermute | solution.py:113
  131.2 1.1 collective-permute-start.17
  132.3 0.7 slice.77
  133.5 0.7 slice.76
  134.3 2.0 collective-permute-done.18.refs_9_
  136.3 0.7 copy-done.7
  137.8 1.4 collective-permute-done.10.refs_4_
  139.2 4.8 %collective-permute-done.9.refs_3_ = bf16[2,2,32,1024]{3,2,1,0:T(8,128)(2,1)} collective-permute-done((bf16[2,2,32,1024]{3,2,1,0:T(8,128)(2,1)}, bf16[2,2,32,1024]{3,2,1,0:T(8,128)(2,1)}, u32[]{:S(2)}, u32[]{:S(2)}) %collective-permute-start.9) | collective-permute-done | bytes 262176 | tf_op jit(solution)/shard_map/ppermute | solution.py:113
  144.0 19.7 %shard_map.101 = (bf16[4,512,512]{2,1,0:T(8,128)(2,1)}, bf16[4,512,512]{2,1,0:T(8,128)(2,1)}, bf16[512,1024]{1,0:T(8,128)(2,1)}, bf16[512,1024]{1,0:T(8,128)(2,1)}) custom-call(s32[2]{0:T(128)} %pad_add_fusion.place, bf16[32,16,2048]{2,1,0:T(8,128)(2,1)} %all-to-all-done.x0, bf16[32,16,2048]{2,1,0:T(8,128)(2,1)} %collective-permute-done.x1, ...), custom_call_target="tpu_custom_call" | custom-call | flops 8999999488 | bytes 18874368 | tf_op jit(solution)/shard_map/pallas_call | solution.py:150
  163.7 6.9 %collective-permute-start.19 = (bf16[4,512,512]{2,1,0:T(8,128)(2,1)}, bf16[4,512,512]{2,1,0:T(8,128)(2,1)S(1)}, u32[]{:S(2)}, u32[]{:S(2)}) collective-permute-start(bf16[4,512,512]{2,1,0:T(8,128)(2,1)} %get-tuple-element.10), channel_id=1, source_target_pairs={{0,128},{128,0},{1,129},{129,1},{2,130},{130,2},{3,131},{131,3},{4... | collective-permute-start | bytes 6291464 | tf_op jit(solution)/shard_map/ppermute | solution.py:113
  170.7 4.0 %collective-permute-done.19 = bf16[4,512,512]{2,1,0:T(8,128)(2,1)S(1)} collective-permute-done((bf16[4,512,512]{2,1,0:T(8,128)(2,1)}, bf16[4,512,512]{2,1,0:T(8,128)(2,1)S(1)}, u32[]{:S(2)}, u32[]{:S(2)}) %collective-permute-start.19) | collective-permute-done | bytes 2097184 | tf_op jit(solution)/shard_map/ppermute | solution.py:113
  174.7 3.5 %add_convert_fusion = bf16[4,512,512]{2,1,0:T(8,128)(2,1)} fusion(bf16[4,512,512]{2,1,0:T(8,128)(2,1)S(1)} %collective-permute-done.19, bf16[4,512,512]{2,1,0:T(8,128)(2,1)} %get-tuple-element.9), kind=kLoop, calls=%fused_computation.1 | loop fusion | flops 4194304 | bytes 6291456 | tf_op jit(solution)/shard_map/convert_element_type | solution.py:166
  178.2 50.5 %reduce-scatter.2.cloned.1.call-done = bf16[1,512,512]{2,1,0:T(8,128)(2,1)} async-done(((bf16[4,512,512]{2,1,0:T(8,128)(2,1)}), bf16[1,512,512]{2,1,0:T(8,128)(2,1)}) %reduce-scatter.2.cloned.1.call-update) | async-done | bytes 524304 | tf_op jit(solution)/shard_map/reduce_scatter | solution.py:166
  228.7 7.1 %all-to-all-start.3 = ((bf16[32,16,512]{2,1,0:T(8,128)(2,1)}), bf16[32,16,512]{2,1,0:T(8,128)(2,1)S(1)}, u32[]{:S(2)}, u32[]{:S(2)}) async-start(bf16[32,16,512]{2,1,0:T(8,128)(2,1)} %bitcast.45), calls=%async_computation.4 | async-start | bytes 1048576 | tf_op jit(solution)/shard_map/all_to_all | solution.py:128
  235.8 10.5 %shard_map.102 = bf16[32,2,32,1024]{3,2,1,0:T(8,128)(2,1)} custom-call(bf16[32,16,2048]{2,1,0:T(8,128)(2,1)} %all-to-all-done.x0, bf16[32,16,2048]{2,1,0:T(8,128)(2,1)} %collective-permute-done.x1, bf16[32,16,2048]{2,1,0:T(8,128)(2,1)} %copy-done, bf16[32,16,2048]{2,1,0:T(8,128)(2,1)} %collective-permute-done.1.u1, bf16[512,1024]{1,0:T(8,128)(2,1)} %get-tuple-element.11.d0, ...), custom_call_target="tpu_custom_call" | custom-call | flops 4300000256 | bytes 14680064 | tf_op jit(solution)/shard_map/pallas_call | solution.py:168
  246.3 7.6 %all-to-all-start.4 = ((bf16[32,2,32,1024]{3,2,1,0:T(8,128)(2,1)}), bf16[32,2,32,1024]{3,2,1,0:T(8,128)(2,1)}, u32[]{:S(2)}, u32[]{:S(2)}) async-start(bf16[32,2,32,1024]{3,2,1,0:T(8,128)(2,1)} %shard_map.102), calls=%async_computation.5 | async-start | bytes 8388608 | tf_op jit(solution)/shard_map/all_to_all | solution.py:128
  253.9 51.9 %all-to-all-done.4 = bf16[32,2,32,1024]{3,2,1,0:T(8,128)(2,1)} async-done(((bf16[32,2,32,1024]{3,2,1,0:T(8,128)(2,1)}), bf16[32,2,32,1024]{3,2,1,0:T(8,128)(2,1)}, u32[]{:S(2)}, u32[]{:S(2)}) %all-to-all-start.4) | async-done | bytes 4194336 | tf_op jit(solution)/shard_map/all_to_all | solution.py:128
  305.8 3.1 convert_reduce_fusion
  309.0 6.1 %all_to_all.32 = bf16[2,32,1024]{2,1,0:T(8,128)(2,1)S(1)} all-to-all(bf16[2,32,1024]{2,1,0:T(8,128)(2,1)S(1)} %multiply_convert_fusion), channel_id=1, replica_groups=mesh['dp'=2,'y'=4,'z'=2,'x'=4,'heads'=4] {'dp'}, dimensions={0} | all-to-all | bytes 262144 | tf_op jit(solution)/shard_map/all_to_all | solution.py:128
  315.5 0.6 maximum_bitcast_fusion.3
  316.1 0.6 pad_maximum_fusion.5
  316.7 0.6 pad_maximum_fusion.4
  317.3 0.6 pad_maximum_fusion.3
  318.0 0.8 copy.52
  (61 shorter events, 4.6 us)
Async XLA Ops:
  51.1 7.6 %copy-start = (bf16[32,16,2048]{2,1,0:T(8,128)(2,1)}, bf16[32,16,2048]{2,1,0:T(8,128)(2,1)S(1)}, u32[]{:S(2)}) copy-start(bf16[32,16,2048]{2,1,0:T(8,128)(2,1)S(1)} %all_to_all.31.u0) | copy-start | bytes 6291460
  51.1 33.2 %all-to-all-start = ((bf16[32,16,2048]{2,1,0:T(8,128)(2,1)}), bf16[32,16,2048]{2,1,0:T(8,128)(2,1)}, u32[]{:S(2)}, u32[]{:S(2)}) async-start(bf16[32,16,2048]{2,1,0:T(8,128)(2,1)} %bitcast.2), calls=%async_computation | async-start | bytes 4194304 | tf_op jit(solution)/shard_map/all_to_all | solution.py:128
  57.4 171.3 %reduce-scatter.2.cloned.1.call-start = ((), (), s32[]{:S(2)}) async-start(), calls=%async_computation.7 | async-start | bytes 2621440 | tf_op jit(solution)/shard_map/reduce_scatter | solution.py:166
  57.4 30.6 %collective-permute-start.2 = (bf16[2,32,1024]{2,1,0:T(8,128)(2,1)S(1)}, bf16[2,32,1024]{2,1,0:T(8,128)(2,1)S(1)}, u32[]{:S(2)}, u32[]{:S(2)}) collective-permute-start(bf16[2,32,1024]{2,1,0:T(8,128)(2,1)S(1)} %all_to_all.30), channel_id=1, source_target_pairs={{0,16},{16,0},{1,17},{17,1},{2,18},{18,2},{3,19},{19,3},{4,20},{20... | collective-permute-start | bytes 393224 | tf_op jit(solution)/shard_map/ppermute | solution.py:113
  58.7 85.3 %collective-permute-start.1 = (bf16[32,16,2048]{2,1,0:T(8,128)(2,1)S(1)}, bf16[32,16,2048]{2,1,0:T(8,128)(2,1)}, u32[]{:S(2)}, u32[]{:S(2)}) collective-permute-start(bf16[32,16,2048]{2,1,0:T(8,128)(2,1)S(1)} %all_to_all.31.u0), channel_id=1, source_target_pairs={{0,128},{128,0},{1,129},{129,1},{2,130},{130,2},{3,131},{131,3},{4... | collective-permute-start | bytes 6291464 | tf_op jit(solution)/shard_map/ppermute | solution.py:113
  84.2 59.8 %collective-permute-start = (bf16[32,16,2048]{2,1,0:T(8,128)(2,1)}, bf16[32,16,2048]{2,1,0:T(8,128)(2,1)}, u32[]{:S(2)}, u32[]{:S(2)}) collective-permute-start(bf16[32,16,2048]{2,1,0:T(8,128)(2,1)} %all-to-all-done.x0), channel_id=1, source_target_pairs={{0,128},{128,0},{1,129},{129,1},{2,130},{130,2},{3,131},{131,3},{4... | collective-permute-start | bytes 6291464 | tf_op jit(solution)/shard_map/ppermute | solution.py:113
  88.1 5.2 %collective-permute-start.12 = (bf16[2,32,1024]{2,1,0:T(8,128)(2,1)S(1)}, bf16[2,32,1024]{2,1,0:T(8,128)(2,1)S(1)}, u32[]{:S(2)}, u32[]{:S(2)}) collective-permute-start(bf16[2,32,1024]{2,1,0:T(8,128)(2,1)S(1)} %bitcast.48), channel_id=1, source_target_pairs={{0,12},{4,0},{8,4},{12,8},{1,13},{5,1},{9,5},{13,9},{2,14},{6,2},{... | collective-permute-start | bytes 393224 | tf_op jit(solution)/shard_map/ppermute | solution.py:113
  88.5 5.8 %collective-permute-start.11 = (bf16[2,32,1024]{2,1,0:T(8,128)(2,1)S(1)}, bf16[2,32,1024]{2,1,0:T(8,128)(2,1)S(1)}, u32[]{:S(2)}, u32[]{:S(2)}) collective-permute-start(bf16[2,32,1024]{2,1,0:T(8,128)(2,1)S(1)} %bitcast.49), channel_id=1, source_target_pairs={{0,4},{4,8},{8,12},{12,0},{1,5},{5,9},{9,13},{13,1},{2,6},{6,10},{... | collective-permute-start | bytes 393224 | tf_op jit(solution)/shard_map/ppermute | solution.py:113
  93.3 3.1 collective-permute-start.14
  94.3 4.4 %collective-permute-start.13 = (bf16[1,32,1024]{2,1,0:T(8,128)(2,1)S(1)}, bf16[1,32,1024]{2,1,0:T(8,128)(2,1)S(1)}, u32[]{:S(2)}, u32[]{:S(2)}) collective-permute-start(bf16[1,32,1024]{2,1,0:T(8,128)(2,1)S(1)} %slice.78), channel_id=1, source_target_pairs={{0,4},{4,8},{8,12},{12,0},{1,5},{5,9},{9,13},{13,1},{2,6},{6,10},{... | collective-permute-start | bytes 196616 | tf_op jit(solution)/shard_map/ppermute | solution.py:113
  98.8 45.2 %copy-start.1 = (bf16[4,2,32,1024]{3,2,1,0:T(8,128)(2,1)}, bf16[4,2,32,1024]{3,2,1,0:T(8,128)(2,1)S(1)}, u32[]{:S(2)}) copy-start(bf16[4,2,32,1024]{3,2,1,0:T(8,128)(2,1)S(1)} %pad_maximum_fusion.1.refs_5_) | copy-start | bytes 1572868
  98.8 23.4 %collective-permute-start.16 = (bf16[4,2,32,1024]{3,2,1,0:T(8,128)(2,1)S(1)}, bf16[4,2,32,1024]{3,2,1,0:T(8,128)(2,1)S(1)}, u32[]{:S(2)}, u32[]{:S(2)}) collective-permute-start(bf16[4,2,32,1024]{3,2,1,0:T(8,128)(2,1)S(1)} %pad_maximum_fusion.1.refs_5_), channel_id=1, source_target_pairs={{0,96},{32,0},{64,32},{96,64},{1,97},{33,1},{65,33},{97,65},{2,98}... | collective-permute-start | bytes 1572872 | tf_op jit(solution)/shard_map/ppermute | solution.py:113
  102.3 12.8 %collective-permute-start.4 = (bf16[2,32,1024]{2,1,0:T(8,128)(2,1)S(1)}, bf16[2,32,1024]{2,1,0:T(8,128)(2,1)S(1)}, u32[]{:S(2)}, u32[]{:S(2)}) collective-permute-start(bf16[2,32,1024]{2,1,0:T(8,128)(2,1)S(1)} %bitcast.46), channel_id=1, source_target_pairs={{0,96},{32,0},{64,32},{96,64},{1,97},{33,1},{65,33},{97,65},{2,98}... | collective-permute-start | bytes 393224 | tf_op jit(solution)/shard_map/ppermute | solution.py:113
  102.4 14.9 %collective-permute-start.3 = (bf16[2,32,1024]{2,1,0:T(8,128)(2,1)S(1)}, bf16[2,32,1024]{2,1,0:T(8,128)(2,1)S(1)}, u32[]{:S(2)}, u32[]{:S(2)}) collective-permute-start(bf16[2,32,1024]{2,1,0:T(8,128)(2,1)S(1)} %bitcast.47), channel_id=1, source_target_pairs={{0,32},{32,64},{64,96},{96,0},{1,33},{33,65},{65,97},{97,1},{2,34}... | collective-permute-start | bytes 393224 | tf_op jit(solution)/shard_map/ppermute | solution.py:113
  115.1 3.5 %collective-permute-start.6 = (bf16[1,32,1024]{2,1,0:T(8,128)(2,1)S(1)}, bf16[1,32,1024]{2,1,0:T(8,128)(2,1)S(1)}, u32[]{:S(2)}, u32[]{:S(2)}) collective-permute-start(bf16[1,32,1024]{2,1,0:T(8,128)(2,1)S(1)} %slice.75), channel_id=1, source_target_pairs={{0,96},{32,0},{64,32},{96,64},{1,97},{33,1},{65,33},{97,65},{2,98}... | collective-permute-start | bytes 196616 | tf_op jit(solution)/shard_map/ppermute | solution.py:113
  117.3 4.4 %collective-permute-start.5 = (bf16[1,32,1024]{2,1,0:T(8,128)(2,1)S(1)}, bf16[1,32,1024]{2,1,0:T(8,128)(2,1)S(1)}, u32[]{:S(2)}, u32[]{:S(2)}) collective-permute-start(bf16[1,32,1024]{2,1,0:T(8,128)(2,1)S(1)} %slice.74), channel_id=1, source_target_pairs={{0,32},{32,64},{64,96},{96,0},{1,33},{33,65},{65,97},{97,1},{2,34}... | collective-permute-start | bytes 196616 | tf_op jit(solution)/shard_map/ppermute | solution.py:113
  118.6 12.1 %collective-permute-start.15 = (bf16[4,2,32,1024]{3,2,1,0:T(8,128)(2,1)S(1)}, bf16[4,2,32,1024]{3,2,1,0:T(8,128)(2,1)S(1)}, u32[]{:S(2)}, u32[]{:S(2)}) collective-permute-start(bf16[4,2,32,1024]{3,2,1,0:T(8,128)(2,1)S(1)} %pad_maximum_fusion.1.refs_5_), channel_id=1, source_target_pairs={{0,32},{32,64},{64,96},{96,0},{1,33},{33,65},{65,97},{97,1},{2,34}... | collective-permute-start | bytes 1572872 | tf_op jit(solution)/shard_map/ppermute | solution.py:113
  121.8 22.2 %copy-start.2 = (bf16[4,2,32,1024]{3,2,1,0:T(8,128)(2,1)}, bf16[4,2,32,1024]{3,2,1,0:T(8,128)(2,1)S(1)}, u32[]{:S(2)}) copy-start(bf16[4,2,32,1024]{3,2,1,0:T(8,128)(2,1)S(1)} %pad_maximum_fusion.refs_0_) | copy-start | bytes 1572868
  121.8 9.4 %collective-permute-start.8 = (bf16[4,2,32,1024]{3,2,1,0:T(8,128)(2,1)S(1)}, bf16[4,2,32,1024]{3,2,1,0:T(8,128)(2,1)S(1)}, u32[]{:S(2)}, u32[]{:S(2)}) collective-permute-start(bf16[4,2,32,1024]{3,2,1,0:T(8,128)(2,1)S(1)} %pad_maximum_fusion.refs_0_), channel_id=1, source_target_pairs={{0,12},{4,0},{8,4},{12,8},{1,13},{5,1},{9,5},{13,9},{2,14},{6,2},{... | collective-permute-start | bytes 1572872 | tf_op jit(solution)/shard_map/ppermute | solution.py:113
  122.3 14.0 %copy-start.3 = (bf16[4,2,32,1024]{3,2,1,0:T(8,128)(2,1)}, bf16[4,2,32,1024]{3,2,1,0:T(8,128)(2,1)S(1)}, u32[]{:S(2)}) copy-start(bf16[4,2,32,1024]{3,2,1,0:T(8,128)(2,1)S(1)} %collective-permute-done.16.refs_7_) | copy-start | bytes 1572868
  122.3 10.8 %collective-permute-start.7 = (bf16[4,2,32,1024]{3,2,1,0:T(8,128)(2,1)S(1)}, bf16[4,2,32,1024]{3,2,1,0:T(8,128)(2,1)S(1)}, u32[]{:S(2)}, u32[]{:S(2)}) collective-permute-start(bf16[4,2,32,1024]{3,2,1,0:T(8,128)(2,1)S(1)} %pad_maximum_fusion.refs_0_), channel_id=1, source_target_pairs={{0,4},{4,8},{8,12},{12,0},{1,5},{5,9},{9,13},{13,1},{2,6},{6,10},{... | collective-permute-start | bytes 1572872 | tf_op jit(solution)/shard_map/ppermute | solution.py:113
  130.7 5.5 %copy-start.4 = (bf16[4,2,32,1024]{3,2,1,0:T(8,128)(2,1)}, bf16[4,2,32,1024]{3,2,1,0:T(8,128)(2,1)S(1)}, u32[]{:S(2)}) copy-start(bf16[4,2,32,1024]{3,2,1,0:T(8,128)(2,1)S(1)} %collective-permute-done.15.refs_6_) | copy-start | bytes 1572868
  130.7 5.5 %collective-permute-start.18 = (bf16[2,2,32,1024]{3,2,1,0:T(8,128)(2,1)S(1)}, bf16[2,2,32,1024]{3,2,1,0:T(8,128)(2,1)S(1)}, u32[]{:S(2)}, u32[]{:S(2)}) collective-permute-start(bf16[2,2,32,1024]{3,2,1,0:T(8,128)(2,1)S(1)} %slice.81), channel_id=1, source_target_pairs={{0,96},{32,0},{64,32},{96,64},{1,97},{33,1},{65,33},{97,65},{2,98}... | collective-permute-start | bytes 786440 | tf_op jit(solution)/shard_map/ppermute | solution.py:113
  131.2 5.1 %copy-start.5 = (bf16[4,2,32,1024]{3,2,1,0:T(8,128)(2,1)}, bf16[4,2,32,1024]{3,2,1,0:T(8,128)(2,1)S(1)}, u32[]{:S(2)}) copy-start(bf16[4,2,32,1024]{3,2,1,0:T(8,128)(2,1)S(1)} %collective-permute-done.8.refs_2_) | copy-start | bytes 1572868
  131.2 6.6 %collective-permute-start.17 = (bf16[2,2,32,1024]{3,2,1,0:T(8,128)(2,1)S(1)}, bf16[2,2,32,1024]{3,2,1,0:T(8,128)(2,1)}, u32[]{:S(2)}, u32[]{:S(2)}) collective-permute-start(bf16[2,2,32,1024]{3,2,1,0:T(8,128)(2,1)S(1)} %slice.80), channel_id=1, source_target_pairs={{0,32},{32,64},{64,96},{96,0},{1,33},{33,65},{65,97},{97,1},{2,34}... | collective-permute-start | bytes 786440 | tf_op jit(solution)/shard_map/ppermute | solution.py:113
  133.1 3.2 copy-start.6
  133.1 6.1 %collective-permute-start.10 = (bf16[2,2,32,1024]{3,2,1,0:T(8,128)(2,1)}, bf16[2,2,32,1024]{3,2,1,0:T(8,128)(2,1)}, u32[]{:S(2)}, u32[]{:S(2)}) collective-permute-start(bf16[2,2,32,1024]{3,2,1,0:T(8,128)(2,1)} %slice.77), channel_id=1, source_target_pairs={{0,12},{4,0},{8,4},{12,8},{1,13},{5,1},{9,5},{13,9},{2,14},{6,2},{... | collective-permute-start | bytes 786440 | tf_op jit(solution)/shard_map/ppermute | solution.py:113
  136.3 0.7 copy-start.7
  137.0 7.0 %collective-permute-start.9 = (bf16[2,2,32,1024]{3,2,1,0:T(8,128)(2,1)}, bf16[2,2,32,1024]{3,2,1,0:T(8,128)(2,1)}, u32[]{:S(2)}, u32[]{:S(2)}) collective-permute-start(bf16[2,2,32,1024]{3,2,1,0:T(8,128)(2,1)} %slice.76), channel_id=1, source_target_pairs={{0,4},{4,8},{8,12},{12,0},{1,5},{5,9},{9,13},{13,1},{2,6},{6,10},{... | collective-permute-start | bytes 786440 | tf_op jit(solution)/shard_map/ppermute | solution.py:113
  163.7 10.9 %collective-permute-start.19 = (bf16[4,512,512]{2,1,0:T(8,128)(2,1)}, bf16[4,512,512]{2,1,0:T(8,128)(2,1)S(1)}, u32[]{:S(2)}, u32[]{:S(2)}) collective-permute-start(bf16[4,512,512]{2,1,0:T(8,128)(2,1)} %get-tuple-element.10), channel_id=1, source_target_pairs={{0,128},{128,0},{1,129},{129,1},{2,130},{130,2},{3,131},{131,3},{4... | collective-permute-start | bytes 6291464 | tf_op jit(solution)/shard_map/ppermute | solution.py:113
  228.7 17.6 %all-to-all-start.3 = ((bf16[32,16,512]{2,1,0:T(8,128)(2,1)}), bf16[32,16,512]{2,1,0:T(8,128)(2,1)S(1)}, u32[]{:S(2)}, u32[]{:S(2)}) async-start(bf16[32,16,512]{2,1,0:T(8,128)(2,1)} %bitcast.45), calls=%async_computation.4 | async-start | bytes 1048576 | tf_op jit(solution)/shard_map/all_to_all | solution.py:128
  246.3 59.5 %all-to-all-start.4 = ((bf16[32,2,32,1024]{3,2,1,0:T(8,128)(2,1)}), bf16[32,2,32,1024]{3,2,1,0:T(8,128)(2,1)}, u32[]{:S(2)}, u32[]{:S(2)}) async-start(bf16[32,2,32,1024]{3,2,1,0:T(8,128)(2,1)} %shard_map.102), calls=%async_computation.5 | async-start | bytes 8388608 | tf_op jit(solution)/shard_map/all_to_all | solution.py:128
Sparse Core Ops, SparseCore 0:
  178.3 50.3 reduce-scatter.1
